TPU v7x, 32 devices: a whole 2x2x4 slice. The times are simulated.
32 devices in a mesh: ctx: 8 (over y, x, core), tp: 4 (over z).
Axes of the slice: x: 2, y: 2, z: 4, core: 2. Of those that a mesh axis runs over, the one named last changes fastest.
Arguments:
- hidden: bfloat16 [4096, 8192], P('ctx', 'tp'), may hold values from -6 to 6
- queries: bfloat16 [4096, 8192], P('ctx', 'tp'), may hold values from -6.5 to 6.5
- rotated_keys: bfloat16 [4096, 1024], P('ctx', 'tp'), may hold values from -6 to 6
- frozen_value_rows: bfloat16 [4096, 1024], P('ctx', 'tp'), may hold values from -6 to 6
- adapter_a_v: bfloat16 [8192, 16], P('tp'), may hold values from -0.0625 to 0.0625
- value_up_matrix: bfloat16 [16, 1024], P(None, 'tp'), may hold values from -1.5 to 1.5
- adapter_a_o: bfloat16 [8192, 16], P('tp'), may hold values from -0.0625 to 0.0625
- output_up_matrix: bfloat16 [16, 8192], P(None, 'tp'), may hold values from -1.5 to 1.5
- doc_lengths: int32 [16], replicated, may hold values from 1 to 1536, 4096 in all
- pair_slots: int32 [16], replicated, may hold values from 0 to 15, each once
- token_logratio: float32 [4096], P('ctx'), may hold values from -0.6 to 0.6
- out_cotangent: bfloat16 [4096, 8192], P('ctx', 'tp'), may hold values from -6 to 6
- attn_cotangent: bfloat16 [4096, 8192], P('ctx', 'tp'), may hold values from -6 to 6
Outputs:
- attention_output_rows: bfloat16 [4096, 8192], P('ctx', 'tp')
- output_adapter_term: bfloat16 [4096, 8192], P('ctx', 'tp')
- input_adapter_gradient: bfloat16 [4096, 8192], P('ctx', 'tp')
- value_down_gradient: float32 [8192, 16], P('tp')
- value_up_gradient: float32 [16, 1024], P(None, 'tp')
- output_down_gradient: float32 [8192, 16], P('tp')
- output_up_gradient: float32 [16, 8192], P(None, 'tp')
Inputs may be any that keep to these rules, and one draw needn't show every extreme that they name: `doc_lengths`: the lengths sum to 4096, and the longest document has exactly 1536 tokens. `pair_slots`: each value once; the documents with slots 2p and 2p + 1 answer the same prompt, the even slot being the chosen answer and the odd one the rejected answer.
All inputs are finite; a program needn't handle non-finite values.
Results may differ from a plain program's by a relative error of at most 0.022.
Values may be sent and summed in bfloat16 or wider, within the bound.
A program may use at most 128 MiB of HBM per device.

v0:
```python
import math

import jax
import jax.numpy as jnp
from jax import lax
from jax.sharding import PartitionSpec as P

HEADS = 64
KV_HEADS = 8
HD = 128


ADAPTER_SCALE = 2.0
BETA = 0.5
NEG_FILL = -1e30


def from_behind(value, axis, by):
    peers = lax.axis_size(axis)
    pairs = [(i, i + by) for i in range(peers) if 0 <= i + by < peers]
    return lax.ppermute(value, axis, pairs)


def doc_index(positions, doc_ends):
    return jnp.sum((doc_ends[None, :] <= positions[:, None]).astype(jnp.int32), axis=1)


def doc_weights(margins, pair_slots):
    pair_ids = pair_slots // 2
    signs = jnp.where(pair_slots % 2 == 0, 1.0, -1.0).astype(jnp.float32)
    same_pair = (pair_ids[:, None] == pair_ids[None, :]).astype(jnp.float32)
    gaps = jnp.sum(same_pair * (signs * margins)[None, :], axis=1)
    return -BETA * signs * jax.nn.sigmoid(-BETA * gaps)


def lowrank_sum(local_term):
    return lax.psum(local_term, "tp")


def score_block(left, right):
    return lax.dot_general(
        left, right, (((1,), (1,)), ((), ())), preferred_element_type=jnp.float32
    )


def row_contraction(left, right):
    return lax.dot_general(
        left, right, (((0,), (0,)), ((), ())), preferred_element_type=jnp.float32
    )


def shards(
    hidden,
    queries,
    rotated_keys,
    frozen_value_rows,
    adapter_a_v,
    value_up_matrix,
    adapter_a_o,
    output_up_matrix,
    doc_lengths,
    pair_slots,
    token_logratio,
    out_cotangent,
    attn_cotangent,
):
    row_count = hidden.shape[0]
    group_size = HEADS // KV_HEADS
    local_heads = queries.shape[1] // HD
    local_kv = rotated_keys.shape[1] // HD
    doc_count = doc_lengths.shape[0]
    score_scale = 1.0 / math.sqrt(HD)
    first_row = lax.axis_index("ctx") * row_count
    doc_ends = jnp.cumsum(doc_lengths)
    query_pos = first_row + jnp.arange(row_count, dtype=jnp.int32)
    query_doc = doc_index(query_pos, doc_ends)
    key_pos = first_row - 3 * row_count + jnp.arange(4 * row_count, dtype=jnp.int32)
    key_doc = doc_index(key_pos, doc_ends)
    allowed = (
        (query_doc[:, None] == key_doc[None, :])
        & (key_pos[None, :] <= query_pos[:, None])
        & (key_pos[None, :] >= 0)
    )
    live_slots = []
    for slot_index in range(3):
        last_key = (slot_index + 1) * row_count - 1
        live_slots.append((key_doc[last_key] == query_doc[0]) & (key_pos[last_key] >= 0))
    value_down_rows = lowrank_sum(
        jnp.dot(hidden, adapter_a_v, preferred_element_type=jnp.float32)
    ).astype(jnp.bfloat16)
    value_rows = (
        frozen_value_rows.astype(jnp.float32)
        + ADAPTER_SCALE
        * jnp.dot(value_down_rows, value_up_matrix, preferred_element_type=jnp.float32)
    ).astype(jnp.bfloat16)
    own_pair = jnp.stack([rotated_keys, value_rows])
    pieces = [own_pair]
    current = own_pair
    for step_index in range(3):
        current = from_behind(current, "ctx", 1)
        pieces.append(current)
    window = jnp.concatenate(pieces[::-1], axis=1)
    window = window.reshape(2, 4 * row_count, local_kv, HD).transpose(0, 2, 1, 3)
    query_heads = queries.reshape(row_count, local_heads, HD).transpose(1, 0, 2)
    head_ids = jnp.arange(local_heads, dtype=jnp.int32)

    def head_forward(head_index):
        kv_index = head_index // group_size
        query_head = lax.dynamic_index_in_dim(query_heads, head_index, 0, keepdims=False)
        key_head = lax.dynamic_index_in_dim(window[0], kv_index, 0, keepdims=False)
        value_head = lax.dynamic_index_in_dim(window[1], kv_index, 0, keepdims=False)
        scores = score_block(query_head, key_head)
        scores = jnp.where(allowed, scores * score_scale, NEG_FILL)
        row_top = jnp.max(scores, axis=1, keepdims=True)
        exponent = jnp.exp(scores - row_top)
        attention = (exponent / jnp.sum(exponent, axis=1, keepdims=True)).astype(jnp.bfloat16)
        output = jnp.dot(attention, value_head, preferred_element_type=jnp.float32)
        return (attention, output.astype(jnp.bfloat16))

    def head_backward(attention, grad_head):
        return row_contraction(attention, grad_head)

    stored, outputs = lax.map(head_forward, head_ids)
    onehot = (query_doc[:, None] == jnp.arange(doc_count, dtype=jnp.int32)[None, :]).astype(
        jnp.float32
    )
    margins = lax.psum(jnp.sum(onehot * token_logratio[:, None], axis=0), "ctx")
    token_weight = jnp.sum(onehot * doc_weights(margins, pair_slots)[None, :], axis=1)
    output_gradient_rows = (token_weight[:, None] * out_cotangent.astype(jnp.float32)).astype(
        jnp.bfloat16
    )
    output_down_row_gradient = (
        ADAPTER_SCALE
        * lowrank_sum(
            jnp.dot(output_gradient_rows, output_up_matrix.T, preferred_element_type=jnp.float32)
        )
    ).astype(jnp.bfloat16)
    attn_grad = (
        token_weight[:, None] * attn_cotangent.astype(jnp.float32)
        + jnp.dot(output_down_row_gradient, adapter_a_o.T, preferred_element_type=jnp.float32)
    ).astype(jnp.bfloat16)
    grad_heads = attn_grad.reshape(row_count, local_heads, HD).transpose(1, 0, 2)
    output_gradient_rows, output_down_row_gradient, grad_heads = (
        output_gradient_rows,
        output_down_row_gradient,
        grad_heads,
    )

    def head_after(operands):
        return head_backward(operands[0], operands[1])

    value_terms = lax.map(head_after, (stored, grad_heads))
    attention_output_rows = outputs.transpose(1, 0, 2).reshape(row_count, local_heads * HD)
    value_window = jnp.sum(value_terms.reshape(local_kv, group_size, 4 * row_count, HD), axis=1)
    value_window = value_window.transpose(1, 0, 2).reshape(4 * row_count, local_kv * HD)
    slot_terms = [
        value_window[slot_index * row_count : (slot_index + 1) * row_count]
        for slot_index in range(4)
    ]
    carried = slot_terms[0]
    for step_index in range(1, 4):
        carried = from_behind(carried, "ctx", -1) + slot_terms[step_index]
    value_gradient_rows = carried.astype(jnp.bfloat16)
    output_down_rows = lowrank_sum(
        jnp.dot(attention_output_rows, adapter_a_o, preferred_element_type=jnp.float32)
    ).astype(jnp.bfloat16)
    output_adapter_term = (
        ADAPTER_SCALE
        * jnp.dot(output_down_rows, output_up_matrix, preferred_element_type=jnp.float32)
    ).astype(jnp.bfloat16)
    value_down_row_gradient = (
        ADAPTER_SCALE
        * lowrank_sum(
            jnp.dot(value_gradient_rows, value_up_matrix.T, preferred_element_type=jnp.float32)
        )
    ).astype(jnp.bfloat16)
    input_adapter_gradient = jnp.dot(
        value_down_row_gradient, adapter_a_v.T, preferred_element_type=jnp.float32
    ).astype(jnp.bfloat16)
    local_a_v = row_contraction(hidden, value_down_row_gradient)
    local_value_up = ADAPTER_SCALE * row_contraction(value_down_rows, value_gradient_rows)
    local_a_o = row_contraction(attention_output_rows, output_down_row_gradient)
    local_output_up = ADAPTER_SCALE * row_contraction(output_down_rows, output_gradient_rows)
    value_down_gradient, value_up_gradient, output_down_gradient, output_up_gradient = (
        lax.psum(local_a_v.astype(jnp.bfloat16), "ctx").astype(jnp.float32),
        lax.psum(local_value_up.astype(jnp.bfloat16), "ctx").astype(jnp.float32),
        lax.psum(local_a_o.astype(jnp.bfloat16), "ctx").astype(jnp.float32),
        lax.psum(local_output_up.astype(jnp.bfloat16), "ctx").astype(jnp.float32),
    )
    return (
        attention_output_rows,
        output_adapter_term,
        input_adapter_gradient,
        value_down_gradient,
        value_up_gradient,
        output_down_gradient,
        output_up_gradient,
    )


def solution(mesh):
    in_specs = (
        P("ctx", "tp"),
        P("ctx", "tp"),
        P("ctx", "tp"),
        P("ctx", "tp"),
        P("tp", None),
        P(None, "tp"),
        P("tp", None),
        P(None, "tp"),
        P(),
        P(),
        P("ctx"),
        P("ctx", "tp"),
        P("ctx", "tp"),
    )
    out_specs = (
        P("ctx", "tp"),
        P("ctx", "tp"),
        P("ctx", "tp"),
        P("tp", None),
        P(None, "tp"),
        P("tp", None),
        P(None, "tp"),
    )
    return jax.shard_map(shards, mesh=mesh, in_specs=in_specs, out_specs=out_specs, check_vma=False)
```

profile of v0, /device:TPU:0, one launch (start us, length us, event | category | flops | bytes accessed | tf_op | source)
XLA Modules:
  0.0 477.1 jit_solution(6363900556904162192)
XLA Ops:
  9.2 15.1 %psum.65 = f32[16]{0:T(128)S(1)} all-reduce(f32[16]{0:T(128)S(1)} %select_reduce_fusion.1), channel_id=1, replica_groups=mesh['ctx'=8,'tp'=4] {'ctx'}, use_global_device_ids=true, to_apply=%region_10.11 | all-reduce | flops 16 | bytes 128 | tf_op jit(solution)/shard_map/psum | solution.py:127
  28.3 19.9 %all-reduce.1 = (bf16[512,16]{0,1:T(8,128)(2,1)S(1)}, f32[512,16]{0,1:T(8,128)S(1)}) all-reduce(f32[512,16]{0,1:T(8,128)S(1)} %fusion.40, f32[512,16]{0,1:T(8,128)S(1)} %fusion.26), channel_id=1, replica_groups=mesh['ctx'=8,'tp'=4] {'tp'}, use_global_device_ids=true, to_apply=%region_0.0 | all-reduce | flops 16384 | bytes 114688 | tf_op jit(solution)/shard_map/psum | solution.py:37
  51.5 6.9 %collective-permute-start.1 = (bf16[2,512,256]{2,1,0:T(8,128)(2,1)S(1)}, bf16[2,512,256]{2,1,0:T(8,128)(2,1)}, u32[]{:S(2)}, u32[]{:S(2)}) collective-permute-start(bf16[2,512,256]{2,1,0:T(8,128)(2,1)S(1)} %collective-permute-done), channel_id=1, source_target_pairs={{0,4},{4,8},{8,12},{12,16},{16,20},{20,24},{24,28},{1,5},{5,9},{9,... | collective-permute-start | bytes 1572872 | tf_op jit(solution)/shard_map/ppermute | solution.py:21
  58.4 3.9 copy.40
  62.3 5.7 %collective-permute-start.2 = (bf16[2,512,256]{2,1,0:T(8,128)(2,1)}, bf16[2,512,256]{2,1,0:T(8,128)(2,1)S(1)}, u32[]{:S(2)}, u32[]{:S(2)}) collective-permute-start(bf16[2,512,256]{2,1,0:T(8,128)(2,1)} %collective-permute-done.1), channel_id=1, source_target_pairs={{0,4},{4,8},{8,12},{12,16},{16,20},{20,24},{24,28},{1,5},{5,9},{9,... | collective-permute-start | bytes 1572872 | tf_op jit(solution)/shard_map/ppermute | solution.py:21
  72.4 2.3 bitcast_bitcast_fusion.1
  74.7 207.5 %while.26 = (s32[]{:T(128)}, bf16[16,512,2048]{2,1,0:T(8,128)(2,1)}, bf16[16,512,128]{2,1,0:T(8,128)(2,1)}, s32[16]{0:T(128)S(1)}, bf16[16,512,128]{1,2,0:T(8,12...) while((s32[]{:T(128)}, ...), condition=%wide.region_7.8_spmd.clone, body=%wide.region_4.7_spmd.clone.sunk | while | flops 549518336 | bytes 24413580 | solution.py:123
  80.9 2.6 fusion.78
  93.9 2.6 fusion.78
  106.8 2.6 fusion.78
  119.8 2.6 fusion.78
  132.8 2.6 fusion.78
  145.8 2.6 fusion.78
  158.7 2.6 fusion.78
  171.7 2.6 fusion.78
  184.7 2.6 fusion.78
  197.7 2.6 fusion.78
  210.6 2.6 fusion.78
  223.5 2.6 fusion.78
  236.5 2.6 fusion.78
  249.5 2.6 fusion.78
  262.5 2.6 fusion.78
  275.5 2.6 fusion.78
  282.3 53.2 %while.25 = (s32[]{:T(128)}, f32[16,2048,128]{2,1,0:T(8,128)}, bf16[16,512,2048]{2,1,0:T(8,128)(2,1)}, bf16[16,512,128]{2,1,0:T(8,128)(2,1)}, s32[]{:T(128)}) while((s32[]{:T(128)}, f32[16,2048,128]{2,1,0:T(8,128)}, bf16[16,512,2048]{2,1,0:T(8,128)(2,1)}, bf16[16,512,128]{2,1,0:T(8,128)(2,1)}, s32[]{:T(128)}) %tuple.71), condition=%wide.region_15.16_spmd, body=%wide.region_14.15_spmd.sunk | while | flops 268435456 | bytes 3278397 | solution.py:152
  282.3 3.3 fusion.74
  285.6 3.3 fusion.74
  288.9 3.3 fusion.74
  292.2 3.4 fusion.74
  295.6 3.3 fusion.74
  298.9 3.3 fusion.74
  302.2 3.3 fusion.74
  305.5 3.3 fusion.74
  308.8 3.3 fusion.74
  312.1 3.4 fusion.74
  315.5 3.3 fusion.74
  318.8 3.3 fusion.74
  322.1 3.3 fusion.74
  325.4 3.4 fusion.74
  328.8 3.3 fusion.74
  332.1 3.3 fusion.74
  335.4 8.1 %bitcast_reduce_fusion = f32[2,2048,128]{2,1,0:T(8,128)} fusion(f32[16,2048,128]{2,1,0:T(8,128)} %get-tuple-element.122), kind=kLoop, calls=%fused_computation.24 | loop fusion | flops 3670016 | bytes 18874368 | tf_op jit(solution)/shard_map/reduce_sum | solution.py:154
  343.6 2.7 fusion.39
  352.0 3.5 collective-permute-done.3
  359.8 7.9 %collective-permute-done.4 = f32[512,256]{0,1:T(8,128)S(1)} collective-permute-done((f32[512,256]{0,1:T(8,128)S(1)}, f32[512,256]{0,1:T(8,128)S(1)}, u32[]{:S(2)}, u32[]{:S(2)}) %collective-permute-start.4) | collective-permute-done | bytes 524320 | tf_op jit(solution)/shard_map/ppermute | solution.py:21
  371.1 7.3 %collective-permute-done.5 = f32[512,256]{0,1:T(8,128)S(1)} collective-permute-done((f32[512,256]{0,1:T(8,128)S(1)}, f32[512,256]{0,1:T(8,128)S(1)}, u32[]{:S(2)}, u32[]{:S(2)}) %collective-permute-start.5) | collective-permute-done | bytes 524320 | tf_op jit(solution)/shard_map/ppermute | solution.py:21
  378.7 16.4 %all-reduce = (bf16[512,16]{0,1:T(8,128)(2,1)S(1)}, f32[512,16]{0,1:T(8,128)S(1)}) all-reduce(f32[512,16]{0,1:T(8,128)S(1)} %fusion.41, f32[512,16]{0,1:T(8,128)S(1)} %fusion.42), channel_id=1, replica_groups=mesh['ctx'=8,'tp'=4] {'tp'}, use_global_device_ids=true, to_apply=%region_8.9 | all-reduce | flops 16384 | bytes 114688 | tf_op jit(solution)/shard_map/psum | solution.py:37
  401.6 20.5 %psum.69 = bf16[16,256]{1,0:T(8,128)(2,1)S(1)} all-reduce(bf16[16,256]{1,0:T(8,128)(2,1)S(1)} %fusion.25), channel_id=1, replica_groups=mesh['ctx'=8,'tp'=4] {'ctx'}, use_global_device_ids=true, to_apply=%region_19.20 | all-reduce | flops 4096 | bytes 16384 | tf_op jit(solution)/shard_map/psum | solution.py:186
  422.7 43.1 %all-reduce.5.cloned.1.call-done = (bf16[2048,16]{0,1:T(8,128)(2,1)}, bf16[2048,16]{0,1:T(8,128)(2,1)}, bf16[16,2048]{1,0:T(8,128)(2,1)}) async-done(((bf16[2048,16]{0,1:T(8,128)(2,1)}, bf16[2048,16]{0,1:T(8,128)(2,1)}, bf16[16,2048]{1,0:T(8,128)(2,1)}), (bf16[2048,16]{0,1:T(8,128)(2,1)}, bf16[2048,16]{0,1:T(8,128)(2,1)}, bf16[16,2048]{1,0:T(8,128)(2,1)})) %all-reduce.5.cloned.1.call-update) | async-done | bytes 196624 | tf_op jit(solution)/shard_map/psum | solution.py:185
  (155 shorter events, 141.8 us)
Async XLA Ops:
  7.2 18.9 %copy-start = (bf16[512,2048]{1,0:T(8,128)(2,1)S(1)}, bf16[512,2048]{1,0:T(8,128)(2,1)}, u32[]{:S(2)}) copy-start(bf16[512,2048]{1,0:T(8,128)(2,1)} %param.17) | copy-start | bytes 6291460
  7.2 20.4 %copy-start.9 = (bf16[16,2048]{1,0:T(8,128)(2,1)S(1)}, bf16[16,2048]{1,0:T(8,128)(2,1)}, u32[]{:S(2)}) copy-start(bf16[16,2048]{1,0:T(8,128)(2,1)} %param.24) | copy-start | bytes 196612
  7.2 458.5 %all-reduce.5.cloned.1.call-start = ((), (), s32[]{:S(2)}) async-start(), calls=%async_computation | async-start | bytes 393216 | tf_op jit(solution)/shard_map/psum | solution.py:185
  24.3 3.3 copy-start.2
  26.1 22.2 %copy-start.8 = (bf16[512,256]{1,0:T(8,128)(2,1)S(1)}, bf16[512,256]{1,0:T(8,128)(2,1)}, u32[]{:S(2)}) copy-start(bf16[512,256]{1,0:T(8,128)(2,1)} %param.20) | copy-start | bytes 786436
  26.1 22.2 %copy-start.10 = (bf16[16,256]{1,0:T(8,128)(2,1)S(1)}, bf16[16,256]{1,0:T(8,128)(2,1)}, u32[]{:S(2)}) copy-start(bf16[16,256]{1,0:T(8,128)(2,1)} %param.22) | copy-start | bytes 24580
  27.6 20.9 %copy-start.5 = (bf16[512,256]{1,0:T(8,128)(2,1)S(1)}, bf16[512,256]{1,0:T(8,128)(2,1)}, u32[]{:S(2)}) copy-start(bf16[512,256]{1,0:T(8,128)(2,1)} %param.19) | copy-start | bytes 786436
  48.6 2.8 collective-permute-start
  51.5 10.9 %collective-permute-start.1 = (bf16[2,512,256]{2,1,0:T(8,128)(2,1)S(1)}, bf16[2,512,256]{2,1,0:T(8,128)(2,1)}, u32[]{:S(2)}, u32[]{:S(2)}) collective-permute-start(bf16[2,512,256]{2,1,0:T(8,128)(2,1)S(1)} %collective-permute-done), channel_id=1, source_target_pairs={{0,4},{4,8},{8,12},{12,16},{16,20},{20,24},{24,28},{1,5},{5,9},{9,... | collective-permute-start | bytes 1572872 | tf_op jit(solution)/shard_map/ppermute | solution.py:21
  58.4 9.7 %copy-start.6 = (bf16[2048,16]{0,1:T(8,128)(2,1)S(1)}, bf16[2048,16]{0,1:T(8,128)(2,1)}, u32[]{:S(2)}) copy-start(bf16[2048,16]{0,1:T(8,128)(2,1)} %param.23) | copy-start | bytes 196612
  62.3 10.1 %collective-permute-start.2 = (bf16[2,512,256]{2,1,0:T(8,128)(2,1)}, bf16[2,512,256]{2,1,0:T(8,128)(2,1)S(1)}, u32[]{:S(2)}, u32[]{:S(2)}) collective-permute-start(bf16[2,512,256]{2,1,0:T(8,128)(2,1)} %collective-permute-done.1), channel_id=1, source_target_pairs={{0,4},{4,8},{8,12},{12,16},{16,20},{20,24},{24,28},{1,5},{5,9},{9,... | collective-permute-start | bytes 1572872 | tf_op jit(solution)/shard_map/ppermute | solution.py:21
  347.2 8.3 %collective-permute-start.3 = (f32[512,256]{0,1:T(8,128)}, f32[512,256]{0,1:T(8,128)}, u32[]{:S(2)}, u32[]{:S(2)}) collective-permute-start(f32[512,256]{0,1:T(8,128)} %bitcast.117), channel_id=1, source_target_pairs={{4,0},{8,4},{12,8},{16,12},{20,16},{24,20},{28,24},{5,1},{9,5},{13... | collective-permute-start | bytes 1572872 | tf_op jit(solution)/shard_map/ppermute | solution.py:21
  356.6 11.1 %collective-permute-start.4 = (f32[512,256]{0,1:T(8,128)S(1)}, f32[512,256]{0,1:T(8,128)S(1)}, u32[]{:S(2)}, u32[]{:S(2)}) collective-permute-start(f32[512,256]{0,1:T(8,128)S(1)} %bitcast_add_fusion.2), channel_id=1, source_target_pairs={{4,0},{8,4},{12,8},{16,12},{20,16},{24,20},{28,24},{5,1},{9,5},{13... | collective-permute-start | bytes 1572872 | tf_op jit(solution)/shard_map/ppermute | solution.py:21
  359.8 11.3 %copy-start.1 = (bf16[512,2048]{1,0:T(8,128)(2,1)}, bf16[512,2048]{1,0:T(8,128)(2,1)S(1)}, u32[]{:S(2)}) copy-start(bf16[512,2048]{1,0:T(8,128)(2,1)S(1)} %copy_bitcast_fusion) | copy-start | bytes 6291460
  367.8 10.6 %copy-start.4 = (f32[512,2,128]{0,2,1:T(8,128)S(1)}, f32[512,2,128]{0,2,1:T(8,128)}, u32[]{:S(2)}) copy-start(f32[512,2,128]{0,2,1:T(8,128)} %copy.49) | copy-start | bytes 1572868
  367.8 10.6 %collective-permute-start.5 = (f32[512,256]{0,1:T(8,128)S(1)}, f32[512,256]{0,1:T(8,128)S(1)}, u32[]{:S(2)}, u32[]{:S(2)}) collective-permute-start(f32[512,256]{0,1:T(8,128)S(1)} %bitcast_add_fusion.1), channel_id=1, source_target_pairs={{4,0},{8,4},{12,8},{16,12},{20,16},{24,20},{28,24},{5,1},{9,5},{13... | collective-permute-start | bytes 1572872 | tf_op jit(solution)/shard_map/ppermute | solution.py:21
  371.1 25.0 %copy-start.7 = (bf16[2048,16]{0,1:T(8,128)(2,1)S(1)}, bf16[2048,16]{0,1:T(8,128)(2,1)}, u32[]{:S(2)}) copy-start(bf16[2048,16]{0,1:T(8,128)(2,1)} %param.21) | copy-start | bytes 196612
  395.1 3.1 copy-start.3
Sparse Core Ops, SparseCore 0:
  401.5 64.1 all-reduce.4
where the time goes:
time: 480 us; the launch traced here: 477 us
  matrix products  130 us (27%)
  blocking collectives  71.9 us (15%)
  other arithmetic  64.9 us (14%)
  waiting for transfers between devices  63.3 us (13%)
  loops' own time  62.5 us (13%)
  local copies, waits for them, and re-layouts  52 us (11%)
  starting transfers between devices  18.2 us (4%)
  between operations  14.3 us (3%)
    another operation x1, loops' own time, shards(): stored, outputs = lax.map(head_forward, head_ids)  62.5 us
    dot_general x20, matrix products, row_contraction(): lax.dot_general(left, right, (((0,), (0,)), ((), ())), preferred_element_...  56.6 us
    psum x1, waiting for transfers between devices, shards(): lax.psum(local_a_v.astype(jnp.bfloat16), 'ctx').astype(jnp.float32)  43.1 us
    dot_general x16, matrix products, score_block(): lax.dot_general(left, right, (((1,), (1,)), ((), ())), preferred_element_...  41.9 us
    psum x2, blocking collectives, lowrank_sum(): return lax.psum(local_term, 'tp')  36.3 us
    dynamic_update_slice x16, other arithmetic, shards(): stored, outputs = lax.map(head_forward, head_ids)  33.7 us
    slice x16, local copies, waits for them, and re-layouts, head_forward(): window[1]  26.9 us
    dot_general x16, matrix products, head_forward(): output = jnp.dot(attention, value_head, preferred_element_type=jnp.float32)  21.9 us
  transfers between devices with their start and end apart: 7, of which 5 were waited for; matrix products, arithmetic and copies ran while one was open for 3% of the time, Pallas kernels for 0%

commit v1 on v0

--- a/solution.py
+++ b/solution.py
@@ -3,6 +3,8 @@
 import jax
 import jax.numpy as jnp
 from jax import lax
+from jax.experimental import pallas as pl
+from jax.experimental.pallas import tpu as pltpu
 from jax.sharding import PartitionSpec as P
 
 HEADS = 64
@@ -47,6 +49,196 @@
     return lax.dot_general(
         left, right, (((0,), (0,)), ((), ())), preferred_element_type=jnp.float32
     )
+
+TILE = 256
+STEP_HEADS = 4
+EXP2_SCALE = 1.4426950408889634 / math.sqrt(HD)
+
+
+def attention_kernel(
+    reach_ref,
+    query_ref,
+    key_ref,
+    value_ref,
+    cot_ref,
+    weight_ref,
+    low_grad_ref,
+    low_grad_t_ref,
+    down_t_ref,
+    start_ref,
+    out_ref,
+    value_grad_ref,
+    low_out_ref,
+    down_grad_ref,
+    bias,
+    scores,
+    weights,
+    value_t,
+    value_acc,
+):
+    step = pl.program_id(0)
+    steps_per_kv = HEADS // KV_HEADS // STEP_HEADS
+    row_count = query_ref.shape[0]
+    window = key_ref.shape[0]
+    tiles = window // TILE
+    query_tiles = row_count // TILE
+
+    @pl.when(step == 0)
+    def _():
+        low_out_ref[...] = jnp.zeros_like(low_out_ref)
+
+        @pl.loop(0, query_tiles)
+        def _(qt):
+            first = reach_ref[2 * qt]
+            lane = pl.ds(pl.multiple_of(qt * TILE, TILE), TILE)
+            starts = start_ref[:, lane]
+            query_pos = (
+                window - row_count + qt * TILE + lax.broadcasted_iota(jnp.int32, (1, TILE), 1)
+            )
+
+            @pl.loop(0, reach_ref[2 * qt + 1])
+            def _(k):
+                key_pos = (first + k) * TILE + lax.broadcasted_iota(
+                    jnp.int32, (TILE, TILE), 0
+                )
+                allowed = (key_pos >= starts) & (key_pos <= query_pos)
+                rows = pl.ds(pl.multiple_of(k * TILE, TILE), TILE)
+                bias[qt, rows, :] = jnp.where(allowed, 0.0, NEG_FILL)
+
+    @pl.when(step % steps_per_kv == 0)
+    def _():
+        value_acc[...] = jnp.zeros_like(value_acc)
+        for k in range(tiles):
+            rows = slice(k * TILE, (k + 1) * TILE)
+            value_t[:, rows] = jnp.transpose(value_ref[rows, :].astype(jnp.float32)).astype(
+                jnp.bfloat16
+            )
+
+    def one_head(qt, first, count, h):
+        rows = pl.ds(pl.multiple_of(qt * TILE, TILE), TILE)
+        columns = pl.ds(pl.multiple_of(h * HD, HD), HD)
+        query = query_ref[rows, columns]
+
+        def key_rows(k):
+            return pl.ds(pl.multiple_of((first + k) * TILE, TILE), TILE)
+
+        top = jnp.full((8, TILE), NEG_FILL, jnp.float32)
+        for k in range(count):
+            span = slice(k * TILE, (k + 1) * TILE)
+            block = score_block(key_ref[key_rows(k), :], query) + bias[qt, span, :]
+            scores[span, :] = block
+            top = jnp.maximum(top, jnp.max(block.reshape(TILE // 8, 8, TILE), axis=0))
+        top = jnp.max(top, axis=0, keepdims=True) * EXP2_SCALE
+        total = jnp.zeros((8, TILE), jnp.float32)
+        output = jnp.zeros((HD, TILE), jnp.float32)
+        for k in range(count):
+            span = slice(k * TILE, (k + 1) * TILE)
+            block = jnp.exp2(scores[span, :] * EXP2_SCALE - top)
+            total = total + jnp.sum(block.reshape(TILE // 8, 8, TILE), axis=0)
+            block = block.astype(jnp.bfloat16)
+            weights[span, :] = block
+            output = output + jnp.dot(
+                value_t[:, key_rows(k)], block, preferred_element_type=jnp.float32
+            )
+        inverse = 1.0 / jnp.sum(total, axis=0, keepdims=True)
+        out_ref[rows, columns] = jnp.transpose(output * inverse).astype(jnp.bfloat16)
+        inverse_rows = jnp.transpose(jnp.broadcast_to(inverse, (HD, TILE)))
+        grad = weight_ref[rows, :] * cot_ref[rows, columns].astype(jnp.float32) + jnp.dot(
+            low_grad_ref[rows, :], down_t_ref[:, columns], preferred_element_type=jnp.float32
+        )
+        grad = (grad * inverse_rows).astype(jnp.bfloat16)
+        for k in range(count):
+            span = slice(k * TILE, (k + 1) * TILE)
+            value_acc[key_rows(k), :] += jnp.dot(
+                weights[span, :], grad, preferred_element_type=jnp.float32
+            )
+
+    @pl.loop(0, query_tiles)
+    def _(qt):
+        first = reach_ref[2 * qt]
+        count = reach_ref[2 * qt + 1]
+        for variant in range(1, tiles + 1):
+
+            @pl.when(count == variant)
+            def _():
+                @pl.loop(0, STEP_HEADS)
+                def _(h):
+                    one_head(qt, first, variant, h)
+
+    low_out_ref[...] += lax.dot_general(
+        down_t_ref[...],
+        out_ref[...],
+        (((1,), (1,)), ((), ())),
+        preferred_element_type=jnp.float32,
+    )
+    down_grad_ref[...] = jnp.dot(
+        low_grad_t_ref[...], out_ref[...], preferred_element_type=jnp.float32
+    )
+
+    @pl.when(step % steps_per_kv == steps_per_kv - 1)
+    def _():
+        value_grad_ref[...] = value_acc[...].astype(value_grad_ref.dtype)
+
+
+def attention(reach, queries, keys, values, cot, weight, low_grad, down_t, starts):
+    row_count, width = queries.shape
+    window = keys.shape[0]
+    rank = low_grad.shape[1]
+    block = STEP_HEADS * HD
+    steps = width // block
+    steps_per_kv = HEADS // KV_HEADS // STEP_HEADS
+    by_step = lambda i, reach: (0, i)
+    by_kv = lambda i, reach: (0, i // steps_per_kv)
+    whole = lambda i, reach: (0, 0)
+    return pl.pallas_call(
+        attention_kernel,
+        grid_spec=pltpu.PrefetchScalarGridSpec(
+            num_scalar_prefetch=1,
+            grid=(steps,),
+            in_specs=[
+                pl.BlockSpec((row_count, block), by_step),
+                pl.BlockSpec((window, HD), by_kv),
+                pl.BlockSpec((window, HD), by_kv),
+                pl.BlockSpec((row_count, block), by_step),
+                pl.BlockSpec((row_count, 1), whole),
+                pl.BlockSpec((row_count, rank), whole),
+                pl.BlockSpec((rank, row_count), whole),
+                pl.BlockSpec((rank, block), by_step),
+                pl.BlockSpec((1, row_count), whole),
+            ],
+            out_specs=[
+                pl.BlockSpec((row_count, block), by_step),
+                pl.BlockSpec((window, HD), by_kv),
+                pl.BlockSpec((rank, row_count), whole),
+                pl.BlockSpec((rank, block), by_step),
+            ],
+            scratch_shapes=[
+                pltpu.VMEM((row_count // TILE, window, TILE), jnp.float32),
+                pltpu.VMEM((window, TILE), jnp.float32),
+                pltpu.VMEM((window, TILE), jnp.bfloat16),
+                pltpu.VMEM((HD, window), jnp.bfloat16),
+                pltpu.VMEM((window, HD), jnp.float32),
+            ],
+        ),
+        out_shape=[
+            jax.ShapeDtypeStruct((row_count, width), jnp.bfloat16),
+            jax.ShapeDtypeStruct(keys.shape, jnp.bfloat16),
+            jax.ShapeDtypeStruct((rank, row_count), jnp.float32),
+            jax.ShapeDtypeStruct((rank, width), jnp.float32),
+        ],
+        compiler_params=pltpu.CompilerParams(vmem_limit_bytes=40 * 1024 * 1024),
+    )(reach, queries, keys, values, cot, weight, low_grad, low_grad.T, down_t, starts)
+
+
+def tile_reach(first_row, row_count, doc_ends):
+    query_pos = first_row + jnp.arange(row_count, dtype=jnp.int32)
+    ended = doc_ends[None, :] <= query_pos[:, None]
+    starts = jnp.max(jnp.where(ended, doc_ends[None, :], 0), axis=1)
+    starts = starts - (first_row - 3 * row_count)
+    firsts = starts[::TILE] // TILE
+    lasts = (3 * row_count) // TILE + jnp.arange(row_count // TILE, dtype=jnp.int32)
+    reach = jnp.stack([firsts, lasts - firsts + 1], axis=1).reshape(-1)
+    return reach.astype(jnp.int32), starts.astype(jnp.int32)[None, :]
 
 
 def shards(
@@ -65,26 +257,12 @@
     attn_cotangent,
 ):
     row_count = hidden.shape[0]
-    group_size = HEADS // KV_HEADS
-    local_heads = queries.shape[1] // HD
-    local_kv = rotated_keys.shape[1] // HD
     doc_count = doc_lengths.shape[0]
-    score_scale = 1.0 / math.sqrt(HD)
     first_row = lax.axis_index("ctx") * row_count
     doc_ends = jnp.cumsum(doc_lengths)
     query_pos = first_row + jnp.arange(row_count, dtype=jnp.int32)
     query_doc = doc_index(query_pos, doc_ends)
-    key_pos = first_row - 3 * row_count + jnp.arange(4 * row_count, dtype=jnp.int32)
-    key_doc = doc_index(key_pos, doc_ends)
-    allowed = (
-        (query_doc[:, None] == key_doc[None, :])
-        & (key_pos[None, :] <= query_pos[:, None])
-        & (key_pos[None, :] >= 0)
-    )
-    live_slots = []
-    for slot_index in range(3):
-        last_key = (slot_index + 1) * row_count - 1
-        live_slots.append((key_doc[last_key] == query_doc[0]) & (key_pos[last_key] >= 0))
+    reach, starts = tile_reach(first_row, row_count, doc_ends)
     value_down_rows = lowrank_sum(
         jnp.dot(hidden, adapter_a_v, preferred_element_type=jnp.float32)
     ).astype(jnp.bfloat16)
@@ -100,27 +278,6 @@
         current = from_behind(current, "ctx", 1)
         pieces.append(current)
     window = jnp.concatenate(pieces[::-1], axis=1)
-    window = window.reshape(2, 4 * row_count, local_kv, HD).transpose(0, 2, 1, 3)
-    query_heads = queries.reshape(row_count, local_heads, HD).transpose(1, 0, 2)
-    head_ids = jnp.arange(local_heads, dtype=jnp.int32)
-
-    def head_forward(head_index):
-        kv_index = head_index // group_size
-        query_head = lax.dynamic_index_in_dim(query_heads, head_index, 0, keepdims=False)
-        key_head = lax.dynamic_index_in_dim(window[0], kv_index, 0, keepdims=False)
-        value_head = lax.dynamic_index_in_dim(window[1], kv_index, 0, keepdims=False)
-        scores = score_block(query_head, key_head)
-        scores = jnp.where(allowed, scores * score_scale, NEG_FILL)
-        row_top = jnp.max(scores, axis=1, keepdims=True)
-        exponent = jnp.exp(scores - row_top)
-        attention = (exponent / jnp.sum(exponent, axis=1, keepdims=True)).astype(jnp.bfloat16)
-        output = jnp.dot(attention, value_head, preferred_element_type=jnp.float32)
-        return (attention, output.astype(jnp.bfloat16))
-
-    def head_backward(attention, grad_head):
-        return row_contraction(attention, grad_head)
-
-    stored, outputs = lax.map(head_forward, head_ids)
     onehot = (query_doc[:, None] == jnp.arange(doc_count, dtype=jnp.int32)[None, :]).astype(
         jnp.float32
     )
@@ -135,24 +292,17 @@
             jnp.dot(output_gradient_rows, output_up_matrix.T, preferred_element_type=jnp.float32)
         )
     ).astype(jnp.bfloat16)
-    attn_grad = (
-        token_weight[:, None] * attn_cotangent.astype(jnp.float32)
-        + jnp.dot(output_down_row_gradient, adapter_a_o.T, preferred_element_type=jnp.float32)
-    ).astype(jnp.bfloat16)
-    grad_heads = attn_grad.reshape(row_count, local_heads, HD).transpose(1, 0, 2)
-    output_gradient_rows, output_down_row_gradient, grad_heads = (
-        output_gradient_rows,
+    attention_output_rows, value_window, low_out_t, down_grad_t = attention(
+        reach,
+        queries,
+        window[0],
+        window[1],
+        attn_cotangent,
+        token_weight[:, None],
         output_down_row_gradient,
-        grad_heads,
-    )
-
-    def head_after(operands):
-        return head_backward(operands[0], operands[1])
-
-    value_terms = lax.map(head_after, (stored, grad_heads))
-    attention_output_rows = outputs.transpose(1, 0, 2).reshape(row_count, local_heads * HD)
-    value_window = jnp.sum(value_terms.reshape(local_kv, group_size, 4 * row_count, HD), axis=1)
-    value_window = value_window.transpose(1, 0, 2).reshape(4 * row_count, local_kv * HD)
+        adapter_a_o.T,
+        starts,
+    )
     slot_terms = [
         value_window[slot_index * row_count : (slot_index + 1) * row_count]
         for slot_index in range(4)
@@ -161,9 +311,7 @@
     for step_index in range(1, 4):
         carried = from_behind(carried, "ctx", -1) + slot_terms[step_index]
     value_gradient_rows = carried.astype(jnp.bfloat16)
-    output_down_rows = lowrank_sum(
-        jnp.dot(attention_output_rows, adapter_a_o, preferred_element_type=jnp.float32)
-    ).astype(jnp.bfloat16)
+    output_down_rows = lowrank_sum(low_out_t).T.astype(jnp.bfloat16)
     output_adapter_term = (
         ADAPTER_SCALE
         * jnp.dot(output_down_rows, output_up_matrix, preferred_element_type=jnp.float32)
@@ -179,7 +327,7 @@
     ).astype(jnp.bfloat16)
     local_a_v = row_contraction(hidden, value_down_row_gradient)
     local_value_up = ADAPTER_SCALE * row_contraction(value_down_rows, value_gradient_rows)
-    local_a_o = row_contraction(attention_output_rows, output_down_row_gradient)
+    local_a_o = down_grad_t.T
     local_output_up = ADAPTER_SCALE * row_contraction(output_down_rows, output_gradient_rows)
     value_down_gradient, value_up_gradient, output_down_gradient, output_up_gradient = (
         lax.psum(local_a_v.astype(jnp.bfloat16), "ctx").astype(jnp.float32),

time: 480 us -> 237 us (0.49)
  matrix products: 130 us -> 9.13 us
  loops' own time: 62.5 us -> 0 us
  other arithmetic: 64.9 us -> 11 us
  local copies, waits for them, and re-layouts: 52 us -> 4.02 us
  Pallas kernels: 0 us -> 26.1 us
  waiting for transfers between devices: 63.3 us -> 73 us
  blocking collectives: 71.9 us -> 78.9 us
    dot_general x34 -> x0, matrix products: 66.7 us -> none  [the longest x16 41.9 us: score_block(): lax.dot_general(left, right, (((1,), (1,)), ((), ())), preferred_element_...]
    another operation x2 -> x0, loops' own time: 62.5 us -> none  [the longest x1 62.5 us: shards(): stored, outputs = lax.map(head_forward, head_ids)]
    dot_general x20 -> x3, matrix products: 56.6 us -> 2.36 us  [row_contraction(): lax.dot_general(left, right, (((0,), (0,)), ((), ())), preferred_element_...]
    dynamic_update_slice x16 -> x0, other arithmetic: 33.7 us -> none  [shards(): stored, outputs = lax.map(head_forward, head_ids)]
    slice x16 -> x1, local copies, waits for them, and re-layouts: 26.9 us -> 0.1 us  [tile_reach(): firsts = starts[::TILE] // TILE]
    pallas_call x0 -> x1, Pallas kernels: none -> 26.1 us  [attention(): pl.pallas_call(attention_kernel, grid_spec=pltpu.PrefetchScalarGridSpec(n...]
    reduce_sum x17 -> x0, other arithmetic: 19.5 us -> none  [the longest x16 11.4 us: head_forward(): jnp.sum(exponent, axis=1, keepdims=True)]
    ppermute x6, waiting for transfers between devices: 20.2 us -> 31.4 us  [from_behind(): return lax.ppermute(value, axis, pairs)]
  transfers between devices with their start and end apart: 7 -> 7, of which waited for: 5 -> 6; matrix products, arithmetic and copies ran while one was open for 3% -> 1% of each run, Pallas kernels for 0% -> 0%
where the time goes in v1:
time: 237 us; the launch traced here: 238 us
  blocking collectives  78.9 us (33%)
  waiting for transfers between devices  73 us (31%)
  Pallas kernels  26.1 us (11%)
  starting transfers between devices  21.9 us (9%)
  between operations  14.3 us (6%)
  other arithmetic  11 us (5%)
  matrix products  9.13 us (4%)
  local copies, waits for them, and re-layouts  4.02 us (2%)
    psum x1, waiting for transfers between devices, shards(): lax.psum(local_a_v.astype(jnp.bfloat16), 'ctx').astype(jnp.float32)  41.6 us
    psum x2, blocking collectives, lowrank_sum(): return lax.psum(local_term, 'tp')  36.6 us
    ppermute x6, waiting for transfers between devices, from_behind(): return lax.ppermute(value, axis, pairs)  31.4 us
    psum x1, blocking collectives, shards(): lax.psum(local_value_up.astype(jnp.bfloat16), 'ctx').astype(jnp.float32)  27.2 us
    pallas_call x1, Pallas kernels, attention(): pl.pallas_call(attention_kernel, grid_spec=pltpu.PrefetchScalarGridSpec(n...  26.1 us
    ppermute x6, starting transfers between devices, from_behind(): return lax.ppermute(value, axis, pairs)  21.8 us
    psum x1, blocking collectives, shards(): margins = lax.psum(jnp.sum(onehot * token_logratio[:, None], axis=0), 'ctx')  15.1 us
  transfers between devices with their start and end apart: 7, of which 6 were waited for; matrix products, arithmetic and copies ran while one was open for 1% of the time, Pallas kernels for 0%

profile of v1, /device:TPU:0, one launch (start us, length us, event | category | flops | bytes accessed | tf_op | source)
XLA Modules:
  0.0 238.4 jit_solution(6401322457158497049)
XLA Ops:
  7.3 0.9 copy.27
  8.2 0.1 reduce
  8.3 0.1 fusion.9
  8.4 0.8 select_reduce_fusion.1
  9.2 0.7 and_select_fusion
  9.8 15.1 %psum.64 = f32[16]{0:T(128)S(1)} all-reduce(f32[16]{0:T(128)S(1)} %select_reduce_fusion.1), channel_id=1, replica_groups=mesh['ctx'=8,'tp'=4] {'ctx'}, use_global_device_ids=true, to_apply=%region_5.6 | all-reduce | flops 16 | bytes 128 | tf_op jit(solution)/shard_map/psum | solution.py:284
  25.0 0.8 fusion.16
  25.8 0.2 select_reduce_fusion.2
  26.1 1.5 fusion.17
  27.7 0.7 fusion.6
  28.4 19.9 %all-reduce.1 = (bf16[512,16]{0,1:T(8,128)(2,1)S(1)}, f32[512,16]{0,1:T(8,128)S(1)}) all-reduce(f32[512,16]{0,1:T(8,128)S(1)} %fusion.17, f32[512,16]{0,1:T(8,128)S(1)} %fusion.6), channel_id=1, replica_groups=mesh['ctx'=8,'tp'=4] {'tp'}, use_global_device_ids=true, to_apply=%region_2.3 | all-reduce | flops 16384 | bytes 114688 | tf_op jit(solution)/shard_map/psum | solution.py:39
  48.3 0.3 fusion.4
  48.6 0.3 copy-done.13
  49.0 1.3 collective-permute-start
  50.3 1.5 collective-permute-done
  51.8 6.9 %collective-permute-start.1 = (bf16[2,512,256]{2,1,0:T(8,128)(2,1)S(1)}, bf16[2,512,256]{2,1,0:T(8,128)(2,1)}, u32[]{:S(2)}, u32[]{:S(2)}) collective-permute-start(bf16[2,512,256]{2,1,0:T(8,128)(2,1)S(1)} %collective-permute-done), channel_id=1, source_target_pairs={{0,4},{4,8},{8,12},{12,16},{16,20},{20,24},{24,28},{1,5},{5,9},{9,... | collective-permute-start | bytes 1572872 | tf_op jit(solution)/shard_map/ppermute | solution.py:23
  58.6 0.1 slice.21
  58.8 0.8 collective-permute-done.1
  59.5 9.6 %collective-permute-start.2 = (bf16[2,512,256]{2,1,0:T(8,128)(2,1)}, bf16[2,512,256]{2,1,0:T(8,128)(2,1)}, u32[]{:S(2)}, u32[]{:S(2)}) collective-permute-start(bf16[2,512,256]{2,1,0:T(8,128)(2,1)} %collective-permute-done.1), channel_id=1, source_target_pairs={{0,4},{4,8},{8,12},{12,16},{16,20},{20,24},{24,28},{1,5},{5,9},{9,... | collective-permute-start | bytes 1572872 | tf_op jit(solution)/shard_map/ppermute | solution.py:23
  69.2 0.1 copy.28
  69.3 0.1 copy.30.low_grad_ref
  69.5 0.1 copy.29.weight_ref
  69.6 0.8 fusion.30.low_grad_t_ref
  70.4 1.5 maximum_maximum_fusion
  71.9 0.1 slice_bitcast_fusion
  72.1 1.4 copy-done.1
  73.5 0.6 copy-done.2
  74.1 26.1 %shard_map.180 = (bf16[512,2048]{1,0:T(8,128)(2,1)}, bf16[2048,256]{1,0:T(8,128)(2,1)S(1)}, f32[16,512]{1,0:T(8,128)S(1)}, f32[16,2048]{1,0:T(8,128)S(1)}) custom-call(s32[4]{0:T(128)S(1)} %reshape.63.reach_ref, bf16[512,2048]{1,0:T(8,128)(2,1)S(1)} %copy-done.1, bf16[2048,256]{1,0:T(8,128)(2,1)S(1)} %get-tuple-element.29.key_ref, ...), custom_call_target="tpu_custom_call" | custom-call | tf_op jit(solution)/shard_map/pallas_call | solution.py:193
  100.2 1.3 collective-permute-start.3
  101.5 10.2 %collective-permute-done.3 = bf16[512,256]{1,0:T(8,128)(2,1)S(1)} collective-permute-done((bf16[512,256]{1,0:T(8,128)(2,1)S(1)}, bf16[512,256]{1,0:T(8,128)(2,1)S(1)}, u32[]{:S(2)}, u32[]{:S(2)}) %collective-permute-start.3) | collective-permute-done | bytes 262176 | tf_op jit(solution)/shard_map/ppermute | solution.py:23
  111.8 1.4 collective-permute-start.4
  113.2 7.1 %collective-permute-done.4 = bf16[512,256]{1,0:T(8,128)(2,1)S(1)} collective-permute-done((bf16[512,256]{1,0:T(8,128)(2,1)S(1)}, bf16[512,256]{1,0:T(8,128)(2,1)S(1)}, u32[]{:S(2)}, u32[]{:S(2)}) %collective-permute-start.4) | collective-permute-done | bytes 262176 | tf_op jit(solution)/shard_map/ppermute | solution.py:23
  120.4 1.3 collective-permute-start.5
  121.7 0.6 convert_bitcast_fusion
  122.3 11.9 %collective-permute-done.5 = bf16[512,256]{1,0:T(8,128)(2,1)S(1)} collective-permute-done((bf16[512,256]{1,0:T(8,128)(2,1)S(1)}, bf16[512,256]{1,0:T(8,128)(2,1)S(1)}, u32[]{:S(2)}, u32[]{:S(2)}) %collective-permute-start.5) | collective-permute-done | bytes 262176 | tf_op jit(solution)/shard_map/ppermute | solution.py:23
  134.2 0.2 fusion.7
  134.4 16.6 %all-reduce = (bf16[16,512]{1,0:T(8,128)(2,1)S(1)}, f32[512,16]{0,1:T(8,128)S(1)}) all-reduce(f32[16,512]{1,0:T(8,128)} %copy-done.4, f32[512,16]{0,1:T(8,128)S(1)} %fusion.7), channel_id=1, replica_groups=mesh['ctx'=8,'tp'=4] {'tp'}, use_global_device_ids=true, to_apply=%region_9.10 | all-reduce | flops 16384 | bytes 114688 | tf_op jit(solution)/shard_map/psum | solution.py:39
  151.0 1.0 fusion.1
  152.1 2.0 convolution_convert_fusion
  154.1 1.2 fusion
  155.3 2.1 multiply_convert_fusion
  157.4 0.2 fusion.5
  157.6 27.2 %psum.69 = bf16[16,256]{1,0:T(8,128)(2,1)S(1)} all-reduce(bf16[16,256]{1,0:T(8,128)(2,1)S(1)} %fusion.5), channel_id=1, replica_groups=mesh['ctx'=8,'tp'=4] {'ctx'}, use_global_device_ids=true, to_apply=%region_12.13 | all-reduce | flops 4096 | bytes 16384 | tf_op jit(solution)/shard_map/psum | solution.py:334
  184.8 0.6 convert_element_type.81
  185.4 41.6 %all-reduce.5.cloned.1.call-done = (bf16[2048,16]{0,1:T(8,128)(2,1)}, bf16[2048,16]{0,1:T(8,128)(2,1)}, bf16[16,2048]{1,0:T(8,128)(2,1)}) async-done(((bf16[2048,16]{0,1:T(8,128)(2,1)}, bf16[2048,16]{0,1:T(8,128)(2,1)}, bf16[16,2048]{1,0:T(8,128)(2,1)}), (bf16[2048,16]{0,1:T(8,128)(2,1)}, bf16[2048,16]{0,1:T(8,128)(2,1)}, bf16[16,2048]{1,0:T(8,128)(2,1)})) %all-reduce.5.cloned.1.call-update) | async-done | bytes 196624 | tf_op jit(solution)/shard_map/psum | solution.py:333
  227.0 1.5 convert_element_type.79
  228.5 1.5 convert_element_type.84
  230.0 1.5 convert_element_type.86
  (51 shorter events, 0.5 us)
Async XLA Ops:
  7.2 18.9 %copy-start = (bf16[512,2048]{1,0:T(8,128)(2,1)S(1)}, bf16[512,2048]{1,0:T(8,128)(2,1)}, u32[]{:S(2)}) copy-start(bf16[512,2048]{1,0:T(8,128)(2,1)} %param.13) | copy-start | bytes 6291460
  7.2 20.4 %copy-start.11 = (bf16[16,2048]{1,0:T(8,128)(2,1)S(1)}, bf16[16,2048]{1,0:T(8,128)(2,1)}, u32[]{:S(2)}) copy-start(bf16[16,2048]{1,0:T(8,128)(2,1)} %param.20) | copy-start | bytes 196612
  7.2 219.8 %all-reduce.5.cloned.1.call-start = ((), (), s32[]{:S(2)}) async-start(), calls=%async_computation | async-start | bytes 393216 | tf_op jit(solution)/shard_map/psum | solution.py:333
  25.0 2.7 %copy-start.5 = (bf16[512,2048]{1,0:T(8,128)(2,1)S(1)}, bf16[512,2048]{1,0:T(8,128)(2,1)}, u32[]{:S(2)}) copy-start(bf16[512,2048]{1,0:T(8,128)(2,1)} %param.24) | copy-start | bytes 6291460
  26.1 43.4 %copy-start.15 = (f32[512]{0:T(512)}, f32[512]{0:T(512)S(1)}, u32[]{:S(2)}) copy-start(f32[512]{0:T(512)S(1)} %select_reduce_fusion) | copy-start | bytes 6148
  26.1 22.2 %copy-start.9 = (bf16[512,256]{1,0:T(8,128)(2,1)S(1)}, bf16[512,256]{1,0:T(8,128)(2,1)}, u32[]{:S(2)}) copy-start(bf16[512,256]{1,0:T(8,128)(2,1)} %param.16) | copy-start | bytes 786436
  26.1 22.2 %copy-start.17 = (bf16[16,256]{1,0:T(8,128)(2,1)S(1)}, bf16[16,256]{1,0:T(8,128)(2,1)}, u32[]{:S(2)}) copy-start(bf16[16,256]{1,0:T(8,128)(2,1)} %param.18) | copy-start | bytes 24580
  27.6 21.3 %copy-start.7 = (bf16[512,256]{1,0:T(8,128)(2,1)S(1)}, bf16[512,256]{1,0:T(8,128)(2,1)}, u32[]{:S(2)}) copy-start(bf16[512,256]{1,0:T(8,128)(2,1)} %param.15) | copy-start | bytes 786436
  48.3 0.6 copy-start.13
  48.3 21.0 %copy-start.10 = (f32[512,16]{0,1:T(8,128)}, f32[512,16]{0,1:T(8,128)S(1)}, u32[]{:S(2)}) copy-start(f32[512,16]{0,1:T(8,128)S(1)} %get-tuple-element.20) | copy-start | bytes 98308
  49.0 2.8 %collective-permute-start = (bf16[2,512,256]{2,1,0:T(8,128)(2,1)S(1)}, bf16[2,512,256]{2,1,0:T(8,128)(2,1)S(1)}, u32[]{:S(2)}, u32[]{:S(2)}) collective-permute-start(bf16[2,512,256]{2,1,0:T(8,128)(2,1)S(1)} %pad_maximum_fusion), channel_id=1, source_target_pairs={{0,4},{4,8},{8,12},{12,16},{16,20},{20,24},{24,28},{1,5},{5,9},{9,... | collective-permute-start | bytes 1572872 | tf_op jit(solution)/shard_map/ppermute | solution.py:23
  51.8 7.7 %collective-permute-start.1 = (bf16[2,512,256]{2,1,0:T(8,128)(2,1)S(1)}, bf16[2,512,256]{2,1,0:T(8,128)(2,1)}, u32[]{:S(2)}, u32[]{:S(2)}) collective-permute-start(bf16[2,512,256]{2,1,0:T(8,128)(2,1)S(1)} %collective-permute-done), channel_id=1, source_target_pairs={{0,4},{4,8},{8,12},{12,16},{16,20},{20,24},{24,28},{1,5},{5,9},{9,... | collective-permute-start | bytes 1572872 | tf_op jit(solution)/shard_map/ppermute | solution.py:23
  59.5 10.9 %collective-permute-start.2 = (bf16[2,512,256]{2,1,0:T(8,128)(2,1)}, bf16[2,512,256]{2,1,0:T(8,128)(2,1)}, u32[]{:S(2)}, u32[]{:S(2)}) collective-permute-start(bf16[2,512,256]{2,1,0:T(8,128)(2,1)} %collective-permute-done.1), channel_id=1, source_target_pairs={{0,4},{4,8},{8,12},{12,16},{16,20},{20,24},{24,28},{1,5},{5,9},{9,... | collective-permute-start | bytes 1572872 | tf_op jit(solution)/shard_map/ppermute | solution.py:23
  70.4 1.7 copy-start.3
  71.9 1.6 copy-start.1
  71.9 2.2 copy-start.2
  100.2 22.1 %copy-start.4 = (f32[16,512]{1,0:T(8,128)}, f32[16,512]{1,0:T(8,128)S(1)}, u32[]{:S(2)}) copy-start(f32[16,512]{1,0:T(8,128)S(1)} %get-tuple-element.12) | copy-start | bytes 98308
  100.2 34.0 %copy-start.18 = (bf16[16,256]{1,0:T(8,128)(2,1)S(1)}, bf16[16,256]{1,0:T(8,128)(2,1)}, u32[]{:S(2)}) copy-start(bf16[16,256]{1,0:T(8,128)(2,1)} %param.18) | copy-start | bytes 24580
  100.2 11.5 %collective-permute-start.3 = (bf16[512,256]{1,0:T(8,128)(2,1)S(1)}, bf16[512,256]{1,0:T(8,128)(2,1)S(1)}, u32[]{:S(2)}, u32[]{:S(2)}) collective-permute-start(bf16[512,256]{1,0:T(8,128)(2,1)S(1)} %slice.24), channel_id=1, source_target_pairs={{4,0},{8,4},{12,8},{16,12},{20,16},{24,20},{28,24},{5,1},{9,5},{13... | collective-permute-start | bytes 786440 | tf_op jit(solution)/shard_map/ppermute | solution.py:23
  111.8 40.3 %copy-start.8 = (bf16[2048,16]{0,1:T(8,128)(2,1)S(1)}, bf16[2048,16]{0,1:T(8,128)(2,1)}, u32[]{:S(2)}) copy-start(bf16[2048,16]{0,1:T(8,128)(2,1)} %param.17) | copy-start | bytes 196612
  111.8 8.6 %collective-permute-start.4 = (bf16[512,256]{1,0:T(8,128)(2,1)S(1)}, bf16[512,256]{1,0:T(8,128)(2,1)S(1)}, u32[]{:S(2)}, u32[]{:S(2)}) collective-permute-start(bf16[512,256]{1,0:T(8,128)(2,1)S(1)} %slice_add_fusion.2), channel_id=1, source_target_pairs={{4,0},{8,4},{12,8},{16,12},{20,16},{24,20},{28,24},{5,1},{9,5},{13... | collective-permute-start | bytes 786440 | tf_op jit(solution)/shard_map/ppermute | solution.py:23
  120.4 13.8 %collective-permute-start.5 = (bf16[512,256]{1,0:T(8,128)(2,1)S(1)}, bf16[512,256]{1,0:T(8,128)(2,1)S(1)}, u32[]{:S(2)}, u32[]{:S(2)}) collective-permute-start(bf16[512,256]{1,0:T(8,128)(2,1)S(1)} %slice_add_fusion.1), channel_id=1, source_target_pairs={{4,0},{8,4},{12,8},{16,12},{20,16},{24,20},{28,24},{5,1},{9,5},{13... | collective-permute-start | bytes 786440 | tf_op jit(solution)/shard_map/ppermute | solution.py:23
  151.0 3.1 %copy-start.6 = (bf16[512,2048]{1,0:T(8,128)(2,1)S(1)}, bf16[512,2048]{1,0:T(8,128)(2,1)}, u32[]{:S(2)}) copy-start(bf16[512,2048]{1,0:T(8,128)(2,1)} %param.24) | copy-start | bytes 6291460
  151.0 3.1 %copy-start.16 = (f32[512]{0:T(512)S(1)}, f32[512]{0:T(512)}, u32[]{:S(2)}) copy-start(f32[512]{0:T(512)} %copy-done.15) | copy-start | bytes 6148
  154.1 1.2 copy-start.12
  154.1 3.3 %copy-start.14 = (bf16[512,16]{0,1:T(8,128)(2,1)S(1)}, bf16[512,16]{0,1:T(8,128)(2,1)}, u32[]{:S(2)}) copy-start(bf16[512,16]{0,1:T(8,128)(2,1)} %copy-done.13) | copy-start | bytes 49156
Sparse Core Ops, SparseCore 0:
  157.5 69.4 all-reduce.4
